TPU v7x, 32 devices: a whole 2x2x4 slice. The times are simulated.
32 devices in a mesh: logger: 4 (over y, x), seq: 2 (over core), vocab: 4 (over z).
Axes of the slice: x: 2, y: 2, z: 4, core: 2. Of those that a mesh axis runs over, the one named last changes fastest.
Arguments:
- hidden: bfloat16 [4, 64, 4096], P('logger', ('seq', 'vocab'))
- head_weight: bfloat16 [4, 4096, 4096], P('logger', None, ('seq', 'vocab')), may hold values from -0.09375 to 0.09375
- logged_tokens: int32 [64], replicated, may hold values from 0 to 4095
- logger_share: float32 [4], replicated, may hold values from 0.1 to 1
Outputs:
- log_weight: float32 [4, 64], P('logger', ('seq', 'vocab'))
All inputs are finite; a program needn't handle non-finite values.
Results may differ from a plain program's by a relative error of at most 0.00045.
Values may be sent and summed in bfloat16 or wider, within the bound.
A program may use at most 64 MiB of HBM per device.

v0:
```python
import jax
import jax.numpy as jnp
from jax import lax
from jax.sharding import PartitionSpec as P


def prefix(part, axis, combine, identity):
    place = lax.axis_index(axis)
    gathered = lax.all_gather(part, axis)
    state = jnp.zeros_like(part) + jnp.asarray(identity, part.dtype)

    def one(hop, state):
        return combine(state, lax.dynamic_index_in_dim(gathered, hop, 0, False))

    return lax.fori_loop(0, place, one, state)


def place(buffer, values, start):
    return values


def add_values(earlier, later):
    return earlier + later


def on_device(hidden, head_weight, logged_tokens, logger_share):
    token_rows = hidden[0]
    weight = head_weight[0]
    col_count = weight.shape[1]
    per_device = token_rows.shape[0]
    total_tokens = logged_tokens.shape[0]
    position = lax.axis_index(("seq", "vocab"))
    column_ids = position * col_count + lax.broadcasted_iota(jnp.int32, (1, col_count), 1)
    zeros = jnp.zeros((total_tokens,), jnp.float32)
    start_carry = (zeros, zeros, zeros)
    start = jnp.int32(0)
    logits = jnp.dot(
        lax.all_gather(token_rows, ("seq", "vocab"), axis=0, tiled=True),
        weight,
        preferred_element_type=jnp.float32,
    )
    block_max = jnp.max(logits, axis=1)
    block_sum = jnp.sum(jnp.exp(logits - block_max[:, None]), axis=1)
    block_pick = jnp.sum(jnp.where(logged_tokens[:, None] == column_ids, logits, 0.0), axis=1)
    stats = (
        place(start_carry[0], block_max, start),
        place(start_carry[1], block_sum, start),
        place(start_carry[2], block_pick, start),
    )
    local_max, local_sum, local_pick = stats
    offset = position * per_device
    whole_max = lax.pmax(local_max, ("seq", "vocab"))
    scaled_sum = local_sum * jnp.exp(local_max - whole_max)
    own_sum, own_pick = (
        lax.psum_scatter(scaled_sum, ("seq", "vocab"), scatter_dimension=0, tiled=True),
        lax.psum_scatter(local_pick, ("seq", "vocab"), scatter_dimension=0, tiled=True),
    )
    own_max = lax.dynamic_slice_in_dim(whole_max, offset, per_device)
    logp = own_pick - own_max - jnp.log(own_sum)
    local_cum = jnp.cumsum(logp)
    device_total = jnp.sum(logp)
    earlier_sum = prefix(device_total, ("seq", "vocab"), add_values, jnp.float32(0.0))
    counts = (offset + jnp.arange(per_device) + 1).astype(jnp.float32)
    own_mean = (earlier_sum + local_cum) / counts
    gathered = lax.all_gather(own_mean[None, :], "logger", axis=0, tiled=True)
    prior = jnp.log(logger_share) - jnp.log(jnp.sum(logger_share))
    shifted = prior[:, None] + gathered
    highest = jnp.max(shifted, axis=0)
    mixture = highest + jnp.log(jnp.sum(jnp.exp(shifted - highest[None, :]), axis=0))
    return (own_mean - mixture)[None, :]


def solution(mesh):
    return jax.shard_map(
        on_device,
        mesh=mesh,
        in_specs=(
            P("logger", ("seq", "vocab"), None),
            P("logger", None, ("seq", "vocab")),
            P(),
            P(),
        ),
        out_specs=P("logger", ("seq", "vocab")),
        check_vma=False,
    )
```

profile of v0, /device:TPU:1, one launch (start us, length us, event | category | flops | bytes accessed | tf_op | source)
XLA Modules:
  0.0 94.9 jit_solution(17818057165997192904)
XLA Ops:
  0.0 0.0 copy-start
  0.0 0.0 copy-start.1
  0.0 0.0 copy-start.2
  0.0 28.0 %all-gather = bf16[1,64,4096]{2,1,0:T(8,128)(2,1)S(1)} all-gather(bf16[1,8,4096]{2,1,0:T(8,128)(2,1)} %param.6), channel_id=2, replica_groups=mesh['logger'=4,'seq'=2,'vocab'=4] {'seq','vocab'}, dimensions={1}, use_global_device_ids=true | all-gather | bytes 589824 | tf_op jit(solution)/shard_map/all_gather | solution.py:38
  28.0 3.1 %fusion.7 = (f32[64]{0:T(128)S(1)}, f32[64,512]{1,0:T(8,128)S(1)}) fusion(bf16[1,4096,512]{2,1,0:T(8,128)(2,1)} %param.7, bf16[1,64,4096]{2,1,0:T(8,128)(2,1)S(1)} %all-gather), kind=kOutput, calls=%fused_computation.17 | convolution fusion | flops 268468160 | bytes 4849920 | tf_op jit(solution)/shard_map/dot_general | solution.py:37
  31.1 0.0 copy-done.1
  31.1 0.2 select_reduce_fusion
  31.3 17.5 %pmax.7 = f32[64]{0:T(128)S(1)} all-reduce(f32[64]{0:T(128)S(1)} %get-tuple-element.45), channel_id=1, replica_groups=mesh['logger'=4,'seq'=2,'vocab'=4] {'seq','vocab'}, use_global_device_ids=true, to_apply=%region_3.4 | all-reduce | flops 64 | bytes 512 | tf_op jit(solution)/shard_map/pmax | solution.py:52
  48.9 13.7 %all-reduce.3 = (f32[64]{0:T(128)S(1)}, f32[64]{0:T(128)S(1)}) all-reduce(f32[64]{0:T(128)S(1)} %exponential_multiply_fusion, f32[64]{0:T(128)S(1)} %get-tuple-element.29), channel_id=4, replica_groups=mesh['logger'=4,'seq'=2,'vocab'=4] {'seq','vocab'}, use_global_device_ids=true, to_apply=%region_5.6.clone | all-reduce | flops 128 | bytes 1024
  62.6 0.0 copy-done
  62.6 0.7 fusion.6
  64.0 0.7 fusion.4
  64.7 0.2 reduce-window.4
  64.9 1.4 %dynamic-update-slice = f32[8]{0:T(128)S(1)} dynamic-update-slice(f32[8]{0:T(128)S(1)} %broadcast.48, f32[1]{0:T(128)} %bitcast.3, u32[]{:T(128)} %bitcast.4) | dynamic-update-slice | bytes 12
  66.3 16.3 %all-reduce = f32[8]{0:T(128)S(1)} all-reduce(f32[8]{0:T(128)S(1)} %dynamic-update-slice), channel_id=1, replica_groups=mesh['logger'=4,'seq'=2,'vocab'=4] {'seq','vocab'}, use_global_device_ids=true, to_apply=%add | all-reduce | flops 8 | bytes 64
  82.6 5.1 %while.10 = (s32[]{:T(128)}, f32[]{:T(128)}, s32[]{:T(128)}, f32[8]{0:T(128)S(1)}, s32[]{:T(128)}, /*index=5*/s32[]{:T(128)}, s32[]{:T(128)}) while((s32[]{:T(128)}, f32[]{:T(128)}, s32[]{:T(128)}, f32[8]{0:T(128)S(1)}, s32[]{:T(128)}, /*index=5*/s32[]{:T(128)}, s32[]{:T(128)}) %tuple.22), condition=%wide.region_8.9_spmd, body=%wide.region_7.8_spmd.sunk | while | flops 6 | bytes 143 | solution.py:15
  82.6 0.6 dynamic_slice.11
  83.9 0.6 dynamic_slice.11
  85.2 0.6 dynamic_slice.11
  86.4 0.6 dynamic_slice.11
  87.7 5.2 %all-gather.1 = f32[4,1,8]{2,1,0:T(1,128)S(1)} all-gather(f32[1,1,8]{2,1,0:T(1,128)S(1)} %fusion.8), channel_id=1, replica_groups=mesh['logger'=4,'seq'=2,'vocab'=4] {'logger'}, dimensions={0}, use_global_device_ids=true | all-gather | bytes 160 | tf_op jit(solution)/shard_map/all_gather | solution.py:65
  92.9 0.0 copy-done.2
  92.9 0.6 reduce_sum.48
  94.2 0.1 add_reduce_fusion
  94.3 0.1 exponential_reduce_fusion.1
  94.4 0.5 bitcast_subtract_fusion
  (5 shorter events, 0.0 us)
Async XLA Ops:
  0.0 62.6 %copy-start = (u32[32]{0:T(128)S(1)}, u32[32]{0:T(128)}, u32[]{:S(2)}) copy-start(u32[32]{0:T(128)} %constant.40) | copy-start | bytes 388
  0.0 31.1 %copy-start.1 = (s32[64]{0:T(128)S(1)}, s32[64]{0:T(128)}, u32[]{:S(2)}) copy-start(s32[64]{0:T(128)} %param.8) | copy-start | bytes 772
  0.0 92.9 %copy-start.2 = (f32[4]{0:T(128)S(1)}, f32[4]{0:T(128)}, u32[]{:S(2)}) copy-start(f32[4]{0:T(128)} %param.9) | copy-start | bytes 52
where the time goes:
time: 95.2 us; the launch traced here: 94.9 us
  blocking collectives  80.7 us (85%)
  local copies, waits for them, and re-layouts  4.51 us (5%)
  matrix products  3.13 us (3%)
  loops' own time  2.63 us (3%)
  other arithmetic  2.46 us (3%)
  between operations  1.46 us (2%)
    unnamed x2, blocking collectives  30 us
    all_gather x1, blocking collectives, on_device(): lax.all_gather(token_rows, ('seq', 'vocab'), axis=0, tiled=True)  28 us
    pmax x1, blocking collectives, on_device(): whole_max = lax.pmax(local_max, ('seq', 'vocab'))  17.5 us
    all_gather x1, blocking collectives, on_device(): gathered = lax.all_gather(own_mean[None, :], 'logger', axis=0, tiled=True)  5.16 us
    dot_general x1, matrix products, on_device(): jnp.dot(lax.all_gather(token_rows, ('seq', 'vocab'), axis=0, tiled=True),...  3.13 us
    another operation x1, loops' own time, prefix(): return lax.fori_loop(0, place, one, state)  2.63 us
    dynamic_slice x4, local copies, waits for them, and re-layouts, one(): return combine(state, lax.dynamic_index_in_dim(gathered, hop, 0, False))  2.45 us
    unnamed x9, local copies, waits for them, and re-layouts  2.06 us

commit v1 on v0

--- a/solution.py
+++ b/solution.py
@@ -2,6 +2,27 @@
 import jax.numpy as jnp
 from jax import lax
 from jax.sharding import PartitionSpec as P
+
+
+def collect(shard, axis, dim):
+    peers, place, width = (lax.axis_size(axis), lax.axis_index(axis), shard.shape[dim])
+    forward = [(i, (i + 1) % peers) for i in range(peers)]
+    behind = [(i, (i - 1) % peers) for i in range(peers)]
+    whole = jnp.zeros((*shard.shape[:dim], peers * width, *shard.shape[dim + 1 :]), shard.dtype)
+    whole = lax.dynamic_update_slice_in_dim(whole, shard, place * width, axis=dim)
+    from_left = from_right = shard
+    halfway = peers // 2
+    for step in range(1, halfway + 1):
+        from_left = lax.ppermute(from_left, axis, forward)
+        whole = lax.dynamic_update_slice_in_dim(
+            whole, from_left, (place - step) % peers * width, axis=dim
+        )
+        if step < peers - halfway:
+            from_right = lax.ppermute(from_right, axis, behind)
+            whole = lax.dynamic_update_slice_in_dim(
+                whole, from_right, (place + step) % peers * width, axis=dim
+            )
+    return whole
 
 
 def prefix(part, axis, combine, identity):
@@ -35,9 +56,7 @@
     start_carry = (zeros, zeros, zeros)
     start = jnp.int32(0)
     logits = jnp.dot(
-        lax.all_gather(token_rows, ("seq", "vocab"), axis=0, tiled=True),
-        weight,
-        preferred_element_type=jnp.float32,
+        collect(token_rows, ("seq", "vocab"), 0), weight, preferred_element_type=jnp.float32
     )
     block_max = jnp.max(logits, axis=1)
     block_sum = jnp.sum(jnp.exp(logits - block_max[:, None]), axis=1)

time: 95.2 us -> 89.4 us (0.939)
  blocking collectives: 80.7 us -> 50.1 us
  starting transfers between devices: 0 us -> 12.1 us
  waiting for transfers between devices: 0 us -> 9.96 us
  local copies, waits for them, and re-layouts: 4.51 us -> 6.14 us
    all_gather x1 -> x0, blocking collectives: 28 us -> none  [on_device(): lax.all_gather(token_rows, ('seq', 'vocab'), axis=0, tiled=True)]
    ppermute x0 -> x7, starting transfers between devices: none -> 12.1 us  [the longest x3 9.86 us: collect(): from_right = lax.ppermute(from_right, axis, behind)]
    ppermute x0 -> x7, waiting for transfers between devices: none -> 9.96 us  [the longest x4 9.95 us: collect(): from_left = lax.ppermute(from_left, axis, forward)]
    pmax x1, blocking collectives: 17.5 us -> 13.7 us  [on_device(): whole_max = lax.pmax(local_max, ('seq', 'vocab'))]
    all_gather x1, blocking collectives: 5.16 us -> 6.28 us  [on_device(): gathered = lax.all_gather(own_mean[None, :], 'logger', axis=0, tiled=True)]
    unnamed x9 -> x7, local copies, waits for them, and re-layouts: 2.06 us -> 2.73 us
  transfers between devices with their start and end apart: 0 -> 7, of which waited for: 0 -> 3; matrix products, arithmetic and copies ran while one was open for 0% -> 4% of each run, Pallas kernels for 0% -> 0%
where the time goes in v1:
time: 89.4 us; the launch traced here: 88.5 us
  blocking collectives  50.1 us (56%)
  starting transfers between devices  12.1 us (14%)
  waiting for transfers between devices  9.96 us (11%)
  local copies, waits for them, and re-layouts  6.14 us (7%)
  matrix products  3.13 us (4%)
  other arithmetic  3.12 us (3%)
  loops' own time  2.65 us (3%)
  between operations  1.42 us (2%)
    unnamed x2, blocking collectives  30.1 us
    pmax x1, blocking collectives, on_device(): whole_max = lax.pmax(local_max, ('seq', 'vocab'))  13.7 us
    ppermute x4, waiting for transfers between devices, collect(): from_left = lax.ppermute(from_left, axis, forward)  9.95 us
    ppermute x3, starting transfers between devices, collect(): from_right = lax.ppermute(from_right, axis, behind)  9.86 us
    all_gather x1, blocking collectives, on_device(): gathered = lax.all_gather(own_mean[None, :], 'logger', axis=0, tiled=True)  6.28 us
    dot_general x1, matrix products, on_device(): jnp.dot(collect(token_rows, ('seq', 'vocab'), 0), weight, preferred_eleme...  3.13 us
    unnamed x7, local copies, waits for them, and re-layouts  2.73 us
    another operation x1, loops' own time, prefix(): return lax.fori_loop(0, place, one, state)  2.65 us
  transfers between devices with their start and end apart: 7, of which 3 were waited for; matrix products, arithmetic and copies ran while one was open for 4% of the time, Pallas kernels for 0%

profile of v1, /device:TPU:1, one launch (start us, length us, event | category | flops | bytes accessed | tf_op | source)
XLA Modules:
  0.0 88.5 jit_solution(16486167974854452452)
XLA Ops:
  0.0 2.1 %collective-permute-start = (bf16[8,4096]{1,0:T(8,128)(2,1)}, bf16[8,4096]{1,0:T(8,128)(2,1)S(1)}, u32[]{:S(2)}, u32[]{:S(2)}) collective-permute-start(bf16[8,4096]{1,0:T(8,128)(2,1)} %bitcast.26), channel_id=1, source_target_pairs={{0,1},{1,2},{2,3},{3,4},{4,5},{5,6},{6,7},{7,0},{8,9},{9,10},{10,1... | collective-permute-start | bytes 196616 | tf_op jit(solution)/shard_map/ppermute | solution.py:16
  2.1 2.7 %collective-permute-start.1 = (bf16[8,4096]{1,0:T(8,128)(2,1)}, bf16[8,4096]{1,0:T(8,128)(2,1)S(1)}, u32[]{:S(2)}, u32[]{:S(2)}) collective-permute-start(bf16[8,4096]{1,0:T(8,128)(2,1)} %bitcast.27), channel_id=1, source_target_pairs={{0,7},{1,0},{2,1},{3,2},{4,3},{5,4},{6,5},{7,6},{8,15},{9,8},{10,9... | collective-permute-start | bytes 196616 | tf_op jit(solution)/shard_map/ppermute | solution.py:21
  4.8 1.3 %reduce_sum.48 = f32[]{:T(128)} reduce(f32[4]{0:T(128)} %param.9, f32[]{:T(128)} %constant.67.clone.1), dimensions={0}, to_apply=%region_10.11 | reduce | flops 3 | bytes 24 | tf_op jit(solution)/shard_map/reduce_sum | solution.py:85
  6.1 0.9 constant_dynamic-update-slice_fusion.7
  7.0 1.4 %fusion.5 = (u32[1]{0:T(128)}, u32[1]{0:T(128)}) fusion(u32[32]{0:T(128)} %constant.89, u32[]{:T(128)S(6)} %add.193, u32[]{:T(128)S(6)} %add.196), kind=kLoop, calls=%fused_computation.23 | loop fusion | bytes 24
  9.0 0.0 collective-permute-done
  9.0 0.1 collective-permute-start.2
  9.1 0.0 collective-permute-done.1
  9.1 3.5 %collective-permute-start.3 = (bf16[8,4096]{1,0:T(8,128)(2,1)S(1)}, bf16[8,4096]{1,0:T(8,128)(2,1)S(1)}, u32[]{:S(2)}, u32[]{:S(2)}) collective-permute-start(bf16[8,4096]{1,0:T(8,128)(2,1)S(1)} %collective-permute-done.1), channel_id=1, source_target_pairs={{0,7},{1,0},{2,1},{3,2},{4,3},{5,4},{6,5},{7,6},{8,15},{9,8},{10,9... | collective-permute-start | bytes 196616 | tf_op jit(solution)/shard_map/ppermute | solution.py:21
  12.6 2.5 %collective-permute-done.2 = bf16[8,4096]{1,0:T(8,128)(2,1)S(1)} collective-permute-done((bf16[8,4096]{1,0:T(8,128)(2,1)S(1)}, bf16[8,4096]{1,0:T(8,128)(2,1)S(1)}, u32[]{:S(2)}, u32[]{:S(2)}) %collective-permute-start.2) | collective-permute-done | bytes 65568 | tf_op jit(solution)/shard_map/ppermute | solution.py:16
  15.1 0.0 collective-permute-start.4
  15.1 0.0 collective-permute-done.3
  15.1 3.7 %collective-permute-start.5 = (bf16[8,4096]{1,0:T(8,128)(2,1)S(1)}, bf16[8,4096]{1,0:T(8,128)(2,1)S(1)}, u32[]{:S(2)}, u32[]{:S(2)}) collective-permute-start(bf16[8,4096]{1,0:T(8,128)(2,1)S(1)} %collective-permute-done.3), channel_id=1, source_target_pairs={{0,7},{1,0},{2,1},{3,2},{4,3},{5,4},{6,5},{7,6},{8,15},{9,8},{10,9... | collective-permute-start | bytes 196616 | tf_op jit(solution)/shard_map/ppermute | solution.py:21
  18.8 2.0 %collective-permute-done.4 = bf16[8,4096]{1,0:T(8,128)(2,1)S(1)} collective-permute-done((bf16[8,4096]{1,0:T(8,128)(2,1)S(1)}, bf16[8,4096]{1,0:T(8,128)(2,1)S(1)}, u32[]{:S(2)}, u32[]{:S(2)}) %collective-permute-start.4) | collective-permute-done | bytes 65568 | tf_op jit(solution)/shard_map/ppermute | solution.py:16
  20.9 5.4 %collective-permute-done.6 = bf16[8,4096]{1,0:T(8,128)(2,1)S(1)} collective-permute-done((bf16[8,4096]{1,0:T(8,128)(2,1)S(1)}, bf16[8,4096]{1,0:T(8,128)(2,1)S(1)}, u32[]{:S(2)}, u32[]{:S(2)}) %collective-permute-start.6) | collective-permute-done | bytes 65568 | tf_op jit(solution)/shard_map/ppermute | solution.py:16
  26.3 3.1 %fusion.6 = (f32[64]{0:T(128)S(1)}, f32[64,512]{1,0:T(8,128)S(1)}) fusion(bf16[64,4096]{1,0:T(8,128)(2,1)S(1)} %constant_dynamic-update-slice_fusion, bf16[1,4096,512]{2,1,0:T(8,128)(2,1)} %param.7), kind=kOutput, calls=%fused_computation.24 | convolution fusion | flops 268468160 | bytes 4849920 | tf_op jit(solution)/shard_map/dot_general | solution.py:58
  29.5 13.7 %pmax.7 = f32[64]{0:T(128)S(1)} all-reduce(f32[64]{0:T(128)S(1)} %get-tuple-element.45), channel_id=1, replica_groups=mesh['logger'=4,'seq'=2,'vocab'=4] {'seq','vocab'}, use_global_device_ids=true, to_apply=%region_3.4 | all-reduce | flops 64 | bytes 512 | tf_op jit(solution)/shard_map/pmax | solution.py:71
  43.2 0.2 select_reduce_fusion
  43.4 16.4 %all-reduce.3 = (f32[64]{0:T(128)S(1)}, f32[64]{0:T(128)S(1)}) all-reduce(f32[64]{0:T(128)S(1)} %exponential_multiply_fusion, f32[64]{0:T(128)S(1)} %get-tuple-element.29), channel_id=3, replica_groups=mesh['logger'=4,'seq'=2,'vocab'=4] {'seq','vocab'}, use_global_device_ids=true, to_apply=%region_5.6.clone | all-reduce | flops 128 | bytes 1024
  59.8 0.7 fusion.3
  60.5 1.3 %dynamic-update-slice = f32[8]{0:T(128)S(1)} dynamic-update-slice(f32[8]{0:T(128)S(1)} %broadcast.55, f32[1]{0:T(128)} %bitcast.3, u32[]{:T(128)} %bitcast.4) | dynamic-update-slice | bytes 12
  62.5 13.7 %all-reduce = f32[8]{0:T(128)S(1)} all-reduce(f32[8]{0:T(128)S(1)} %dynamic-update-slice), channel_id=1, replica_groups=mesh['logger'=4,'seq'=2,'vocab'=4] {'seq','vocab'}, use_global_device_ids=true, to_apply=%add | all-reduce | flops 8 | bytes 64
  76.2 5.1 %while.10 = (s32[]{:T(128)}, f32[]{:T(128)}, s32[]{:T(128)}, f32[8]{0:T(128)S(1)}, s32[]{:T(128)}, /*index=5*/s32[]{:T(128)}, s32[]{:T(128)}) while((s32[]{:T(128)}, f32[]{:T(128)}, s32[]{:T(128)}, f32[8]{0:T(128)S(1)}, s32[]{:T(128)}, /*index=5*/s32[]{:T(128)}, s32[]{:T(128)}) %tuple.22), condition=%wide.region_8.9_spmd, body=%wide.region_7.8_spmd.sunk | while | flops 6 | bytes 135 | solution.py:36
  76.2 0.6 dynamic_slice.11
  77.5 0.6 dynamic_slice.11
  78.8 0.6 dynamic_slice.11
  80.1 0.6 dynamic_slice.11
  81.4 0.2 reduce-window.4
  81.6 6.3 %all-gather = f32[4,1,8]{2,1,0:T(1,128)S(1)} all-gather(f32[1,1,8]{2,1,0:T(1,128)S(1)} %fusion.8), channel_id=1, replica_groups=mesh['logger'=4,'seq'=2,'vocab'=4] {'logger'}, dimensions={0}, use_global_device_ids=true | all-gather | bytes 160 | tf_op jit(solution)/shard_map/all_gather | solution.py:84
  87.8 0.1 add_reduce_fusion
  87.9 0.1 exponential_reduce_fusion.1
  88.0 0.5 bitcast_subtract_fusion
  (19 shorter events, 0.1 us)
Async XLA Ops:
  0.0 81.5 %copy-start.1 = (f32[4]{0:T(128)S(1)}, f32[4]{0:T(128)}, u32[]{:S(2)}) copy-start(f32[4]{0:T(128)} %param.9) | copy-start | bytes 52
  0.0 43.2 %copy-start = (s32[64]{0:T(128)S(1)}, s32[64]{0:T(128)}, u32[]{:S(2)}) copy-start(s32[64]{0:T(128)} %param.8) | copy-start | bytes 772
  0.0 9.0 %collective-permute-start = (bf16[8,4096]{1,0:T(8,128)(2,1)}, bf16[8,4096]{1,0:T(8,128)(2,1)S(1)}, u32[]{:S(2)}, u32[]{:S(2)}) collective-permute-start(bf16[8,4096]{1,0:T(8,128)(2,1)} %bitcast.26), channel_id=1, source_target_pairs={{0,1},{1,2},{2,3},{3,4},{4,5},{5,6},{6,7},{7,0},{8,9},{9,10},{10,1... | collective-permute-start | bytes 196616 | tf_op jit(solution)/shard_map/ppermute | solution.py:16
  2.1 6.9 %collective-permute-start.1 = (bf16[8,4096]{1,0:T(8,128)(2,1)}, bf16[8,4096]{1,0:T(8,128)(2,1)S(1)}, u32[]{:S(2)}, u32[]{:S(2)}) collective-permute-start(bf16[8,4096]{1,0:T(8,128)(2,1)} %bitcast.27), channel_id=1, source_target_pairs={{0,7},{1,0},{2,1},{3,2},{4,3},{5,4},{6,5},{7,6},{8,15},{9,8},{10,9... | collective-permute-start | bytes 196616 | tf_op jit(solution)/shard_map/ppermute | solution.py:21
  9.0 6.1 %collective-permute-start.2 = (bf16[8,4096]{1,0:T(8,128)(2,1)S(1)}, bf16[8,4096]{1,0:T(8,128)(2,1)S(1)}, u32[]{:S(2)}, u32[]{:S(2)}) collective-permute-start(bf16[8,4096]{1,0:T(8,128)(2,1)S(1)} %collective-permute-done), channel_id=1, source_target_pairs={{0,1},{1,2},{2,3},{3,4},{4,5},{5,6},{6,7},{7,0},{8,9},{9,10},{10,1... | collective-permute-start | bytes 196616 | tf_op jit(solution)/shard_map/ppermute | solution.py:16
  9.1 6.0 %collective-permute-start.3 = (bf16[8,4096]{1,0:T(8,128)(2,1)S(1)}, bf16[8,4096]{1,0:T(8,128)(2,1)S(1)}, u32[]{:S(2)}, u32[]{:S(2)}) collective-permute-start(bf16[8,4096]{1,0:T(8,128)(2,1)S(1)} %collective-permute-done.1), channel_id=1, source_target_pairs={{0,7},{1,0},{2,1},{3,2},{4,3},{5,4},{6,5},{7,6},{8,15},{9,8},{10,9... | collective-permute-start | bytes 196616 | tf_op jit(solution)/shard_map/ppermute | solution.py:21
  15.1 5.8 %collective-permute-start.4 = (bf16[8,4096]{1,0:T(8,128)(2,1)S(1)}, bf16[8,4096]{1,0:T(8,128)(2,1)S(1)}, u32[]{:S(2)}, u32[]{:S(2)}) collective-permute-start(bf16[8,4096]{1,0:T(8,128)(2,1)S(1)} %collective-permute-done.2), channel_id=1, source_target_pairs={{0,1},{1,2},{2,3},{3,4},{4,5},{5,6},{6,7},{7,0},{8,9},{9,10},{10,1... | collective-permute-start | bytes 196616 | tf_op jit(solution)/shard_map/ppermute | solution.py:16
  15.1 5.8 %collective-permute-start.5 = (bf16[8,4096]{1,0:T(8,128)(2,1)S(1)}, bf16[8,4096]{1,0:T(8,128)(2,1)S(1)}, u32[]{:S(2)}, u32[]{:S(2)}) collective-permute-start(bf16[8,4096]{1,0:T(8,128)(2,1)S(1)} %collective-permute-done.3), channel_id=1, source_target_pairs={{0,7},{1,0},{2,1},{3,2},{4,3},{5,4},{6,5},{7,6},{8,15},{9,8},{10,9... | collective-permute-start | bytes 196616 | tf_op jit(solution)/shard_map/ppermute | solution.py:21
  20.8 5.5 %collective-permute-start.6 = (bf16[8,4096]{1,0:T(8,128)(2,1)S(1)}, bf16[8,4096]{1,0:T(8,128)(2,1)S(1)}, u32[]{:S(2)}, u32[]{:S(2)}) collective-permute-start(bf16[8,4096]{1,0:T(8,128)(2,1)S(1)} %collective-permute-done.4), channel_id=1, source_target_pairs={{0,1},{1,2},{2,3},{3,4},{4,5},{5,6},{6,7},{7,0},{8,9},{9,10},{10,1... | collective-permute-start | bytes 196616 | tf_op jit(solution)/shard_map/ppermute | solution.py:16
